TPU v7x, 512 devices: a whole 4x4x16 slice. The times are simulated.
512 devices in a mesh: row: 16 (over z), col: 32 (over x, y, core).
Axes of the slice: x: 4, y: 4, z: 16, core: 2. Of those that a mesh axis runs over, the one named last changes fastest.
Arguments:
- inverse_top: bfloat16 [4096, 4096], P('col', 'row'), may hold values from -0.09375 to 0.09375
- inverse_one: bfloat16 [6144, 3072], P('col', 'row'), may hold values from -0.109375 to 0.109375
- inverse_two: bfloat16 [8192, 2048], P('col', 'row'), may hold values from -0.125 to 0.125
- inverse_leaf: bfloat16 [8192, 1024], P('col', 'row'), may hold values from -0.1875 to 0.1875
- coupling_one: bfloat16 [3072, 6144], P('row', 'col'), may hold values from -0.109375 to 0.109375
- coupling_two: bfloat16 [2048, 8192], P('row', 'col'), may hold values from -0.125 to 0.125
- coupling_leaf: bfloat16 [1024, 8192], P('row', 'col'), may hold values from -0.1875 to 0.1875
- rhs_top: bfloat16 [4096, 256], P('row', 'col'), may hold values from -6 to 6
- rhs_one: bfloat16 [3072, 512], P('row', 'col'), may hold values from -6 to 6
- rhs_two: bfloat16 [2048, 1024], P('row', 'col'), may hold values from -6 to 6
- rhs_leaf: bfloat16 [1024, 2048], P('row', 'col'), may hold values from -6 to 6
- parent_map_one: int32 [2, 3072], replicated, may hold values from 0 to 4095, as said below
- parent_map_two: int32 [4, 2048], replicated, may hold values from 0 to 6143, as said below
- parent_map_leaf: int32 [8, 1024], replicated, may hold values from 0 to 4095, as said below
Outputs:
- solution_top: bfloat16 [4096, 256], P('row', 'col')
- solution_one: bfloat16 [3072, 512], P('row', 'col')
- solution_two: bfloat16 [2048, 1024], P('row', 'col')
- solution_leaf: bfloat16 [1024, 2048], P('row', 'col')
Inputs may be any that keep to these rules, and one draw needn't show every extreme that they name: `parent_map_one`: row k lists distinct rows of the top front, one for each of the 3072 update rows of front k. Cut the update rows and the top separator each into 16 equal blocks: at most 24 rows of one block land in one block of the top front, a number that is reached in every row, and every block of the top front receives exactly 192 rows from each child. `parent_map_two`: row k lists distinct rows of the front k // 2 of the second level (its 3072 separator rows first, then its 3072 update rows), one for each of the 2048 update rows of front k. Cut the update rows into 16 equal blocks, and the parent's separator rows and its update rows each into 16 equal blocks, block j of the parent being the j-th separator block with the j-th update block: at most 16 rows of one block land in one parent block, reached in every row, and every parent block receives exactly 128 rows from each child. `parent_map_leaf`: as for parent_map_two, one level lower: 1024 update rows of front k into front k // 2 of the third level, at most 8 rows of one block into one parent block, reached in every row, and exactly 64 rows from each child into every parent block.
All inputs are finite; a program needn't handle non-finite values.
Results may differ from a plain program's by a relative error of at most 0.03.
Values may be sent and summed in bfloat16 or wider, within the bound.
No kernel may reach another device: no remote copies, remote signals or barrier semaphores. Data moves between devices by JAX's collectives and lax.ppermute only.
A program may use at most 64 MiB of HBM per device.

v0:
```python
import jax
import jax.numpy as jnp
from jax import lax
from jax.sharding import PartitionSpec as P


def swapped(value, axis, stride):
    mask = 2**stride
    pairs = [(source, source ^ mask) for source in range(lax.axis_size(axis))]
    return lax.ppermute(value, axis, pairs)


def route_tables(mapping, child_index, parent_sep, parent_upd, strips, row_index):
    positions = lax.dynamic_index_in_dim(mapping, child_index, 0, keepdims=False)
    sep_rows = parent_sep // strips
    in_separator = positions < parent_sep
    if parent_upd > 0:
        upd_rows = parent_upd // strips
        target = jnp.where(
            in_separator, positions // sep_rows, (positions - parent_sep) // upd_rows
        )
        offset = jnp.where(
            in_separator, positions % sep_rows, sep_rows + (positions - parent_sep) % upd_rows
        )
    else:
        target = positions // sep_rows
        offset = positions % sep_rows
    block_rows = positions.shape[0] // strips
    blocks = target.reshape(strips, block_rows)
    matches = (blocks[:, :, None] == jnp.arange(strips, dtype=jnp.int32)[None, None, :]).astype(
        jnp.int32
    )
    slot_of = jnp.sum((jnp.cumsum(matches, axis=1) - 1) * matches, axis=2).reshape(-1)
    block_len = sep_rows + parent_upd // strips
    capacity = 2 * positions.shape[0] // (strips * strips)
    source = jnp.arange(positions.shape[0], dtype=jnp.int32) // block_rows
    mine_here = target == row_index
    column_at = jnp.where(mine_here, slot_of, capacity)
    lookup = jnp.full((strips, capacity + 1), block_len, jnp.int32)
    lookup = lookup.at[source, column_at].set(jnp.where(mine_here, offset, block_len))[:, :capacity]
    local_target = lax.dynamic_slice_in_dim(target, row_index * block_rows, block_rows)
    local_slots = lax.dynamic_slice_in_dim(slot_of, row_index * block_rows, block_rows)
    return (local_target, local_slots, lookup, capacity, block_len)


def pack_rows(values, local_target, local_slots, strips, capacity):
    buffer = jnp.zeros((strips, capacity, values.shape[1]), values.dtype)
    return buffer.at[local_target, local_slots].set(values)


def unpack_rows(received, lookup, block_len):
    summed = jnp.zeros((block_len + 1, received.shape[2]), jnp.float32)
    return summed.at[lookup].add(received.astype(jnp.float32))[:block_len]


def spread(portion, depth_bits, pass_on, column):
    for bit_index in range(depth_bits):
        partner = pass_on(portion, bit_index)
        is_upper = column >> bit_index & 1 == 1
        portion = jnp.where(
            is_upper,
            jnp.concatenate([partner, portion], axis=-1),
            jnp.concatenate([portion, partner], axis=-1),
        )
    return portion


def shrink(entire, depth_bits, pass_on, column):
    for bit_index in reversed(range(depth_bits)):
        half_width = entire.shape[-1] // 2
        low_part = entire[..., :half_width]
        high_part = entire[..., half_width:]
        is_upper = column >> bit_index & 1 == 1
        kept_part = jnp.where(is_upper, high_part, low_part)
        sent_part = jnp.where(is_upper, low_part, high_part)
        entire = kept_part + pass_on(sent_part, bit_index)
    return entire


def per_device(
    inverse_top,
    inverse_one,
    inverse_two,
    inverse_leaf,
    coupling_one,
    coupling_two,
    coupling_leaf,
    rhs_top,
    rhs_one,
    rhs_two,
    rhs_leaf,
    parent_map_one,
    parent_map_two,
    parent_map_leaf,
):
    strips = lax.axis_size("row")
    col_count = lax.axis_size("col")
    row_here = lax.axis_index("row")
    column = lax.axis_index("col")
    inverses = [inverse_top, inverse_one, inverse_two, inverse_leaf]
    couplings = [None, coupling_one, coupling_two, coupling_leaf]
    right_sides = [rhs_top, rhs_one, rhs_two, rhs_leaf]
    parent_maps = [None, parent_map_one, parent_map_two, parent_map_leaf]
    orders = [inverse.shape[1] * strips for inverse in inverses]
    groups = [col_count >> tree_level for tree_level in range(4)]
    group_bits = [group_size.bit_length() - 1 for group_size in groups]
    pass_rhs = lambda values, bit_index: swapped(values, "col", bit_index)
    pass_update_sum = lambda values, bit_index: swapped(
        values.astype(jnp.bfloat16), "col", bit_index
    ).astype(values.dtype)
    pass_update_spread = lambda values, bit_index: swapped(values, "col", bit_index)
    pass_solution_sum = lambda values, bit_index: swapped(
        values.astype(jnp.bfloat16), "col", bit_index
    ).astype(values.dtype)
    pass_solution_spread = lambda values, bit_index: swapped(values, "col", bit_index)
    full_rhs = [
        spread(right_sides[tree_level], group_bits[tree_level], pass_rhs, column)
        for tree_level in range(4)
    ]
    own_routes = [None]
    sibling_routes = [None]
    for tree_level in range(1, 4):
        parent_order = orders[tree_level - 1]
        parent_update = parent_order if tree_level > 1 else 0
        front_here = column // groups[tree_level]
        own_routes.append(
            route_tables(
                parent_maps[tree_level], front_here, parent_order, parent_update, strips, row_here
            )
        )
        sibling_routes.append(
            route_tables(
                parent_maps[tree_level],
                front_here ^ 1,
                parent_order,
                parent_update,
                strips,
                row_here,
            )
        )
    pivots = [None] * 4
    incoming = None
    for tree_level in (3, 2, 1, 0):
        sep_rows = inverses[tree_level].shape[1]
        if incoming is None:
            separator = full_rhs[tree_level]
            own_update = None
        else:
            separator = (full_rhs[tree_level].astype(jnp.float32) + incoming[:sep_rows]).astype(
                jnp.bfloat16
            )
            own_update = lax.optimization_barrier(incoming[sep_rows:].astype(jnp.bfloat16))
        partial_value = jnp.dot(inverses[tree_level], separator, preferred_element_type=jnp.float32)
        solved = lax.psum(partial_value.astype(jnp.bfloat16), "row")
        pivots[tree_level] = solved
        if tree_level > 0:
            coupled = jnp.dot(couplings[tree_level], solved, preferred_element_type=jnp.float32)
            reduced = shrink(coupled, group_bits[tree_level], pass_update_sum, column)
            if own_update is None:
                portion = (-reduced).astype(jnp.bfloat16)
            else:
                start_at = column % groups[tree_level] * reduced.shape[1]
                kept_rows = lax.dynamic_slice_in_dim(own_update, start_at, reduced.shape[1], 1)
                portion = (kept_rows.astype(jnp.float32) - reduced).astype(jnp.bfloat16)
            updated = spread(portion, group_bits[tree_level], pass_update_spread, column)
            own_target, own_slots, own_lookup, capacity, block_len = own_routes[tree_level]
            partner = swapped(updated, "col", group_bits[tree_level])
            sib_target, sib_slots, sib_lookup = sibling_routes[tree_level][:3]
            got_own, got_sibling = (
                lax.all_to_all(
                    pack_rows(updated, own_target, own_slots, strips, capacity),
                    "row",
                    split_axis=0,
                    concat_axis=0,
                    tiled=True,
                ),
                lax.all_to_all(
                    pack_rows(partner, sib_target, sib_slots, strips, capacity),
                    "row",
                    split_axis=0,
                    concat_axis=0,
                    tiled=True,
                ),
            )
            incoming = unpack_rows(got_own, own_lookup, block_len) + unpack_rows(
                got_sibling, sib_lookup, block_len
            )
    solutions = [None] * 4
    parent_solution = None
    parent_gathered = None
    for tree_level in range(4):
        solved = pivots[tree_level]
        gathered = None
        if tree_level == 0:
            residual = solved
        else:
            own_target, own_slots, own_lookup, capacity, block_len = own_routes[tree_level]
            pieces = [parent_solution]
            if parent_gathered is not None:
                pieces.append(parent_gathered)
            pieces.append(jnp.zeros((1, parent_solution.shape[1]), jnp.bfloat16))
            parent_rows = jnp.concatenate(pieces, axis=0)
            returned = lax.all_to_all(
                parent_rows[own_lookup], "row", split_axis=0, concat_axis=0, tiled=True
            )
            gathered = returned[own_target, own_slots]
            coupling_term = jnp.dot(
                couplings[tree_level].T, gathered, preferred_element_type=jnp.float32
            )
            residual = (
                solved.astype(jnp.float32)
                - lax.psum(coupling_term.astype(jnp.bfloat16), "row").astype(jnp.float32)
            ).astype(jnp.bfloat16)
        contribution = jnp.dot(inverses[tree_level].T, residual, preferred_element_type=jnp.float32)
        if tree_level == 0:
            summed = lax.psum(contribution.astype(jnp.bfloat16), "col")
            solution = summed
            rhs_width = solution.shape[1] // groups[0]
            solutions[0] = lax.dynamic_slice_in_dim(
                solution, column % groups[0] * rhs_width, rhs_width, 1
            )
        else:
            portion = shrink(
                contribution, group_bits[tree_level], pass_solution_sum, column
            ).astype(jnp.bfloat16)
            solutions[tree_level] = portion
            if tree_level < 3:
                solution = spread(portion, group_bits[tree_level], pass_solution_spread, column)
        parent_solution = solution
        parent_gathered = gathered
    return (solutions[0], solutions[1], solutions[2], solutions[3])


def solution(mesh):
    in_specs = (
        P("col", "row"),
        P("col", "row"),
        P("col", "row"),
        P("col", "row"),
        P("row", "col"),
        P("row", "col"),
        P("row", "col"),
        P("row", "col"),
        P("row", "col"),
        P("row", "col"),
        P("row", "col"),
        P(),
        P(),
        P(),
    )
    out_specs = (P("row", "col"), P("row", "col"), P("row", "col"), P("row", "col"))
    return jax.shard_map(
        per_device, mesh=mesh, in_specs=in_specs, out_specs=out_specs, check_vma=False
    )
```

profile of v0, /device:TPU:1, one launch (start us, length us, event | category | flops | bytes accessed | tf_op | source)
XLA Modules:
  0.0 1660.7 jit_solution(15482872862704650823)
XLA Ops:
  7.2 8.8 collective-permute-start.5
  37.4 9.1 reduce-window.14
  54.5 124.7 %all-reduce.12.cloned.1.call-done = bf16[256,256]{0,1:T(8,128)(2,1)} async-done(((bf16[256,256]{0,1:T(8,128)(2,1)}), bf16[256,256]{0,1:T(8,128)(2,1)}) %all-reduce.12.cloned.1.call-update) | async-done | bytes 131088 | tf_op jit(solution)/shard_map/psum | solution.py:154
  185.4 12.4 collective-permute-start.8
  197.7 4.3 scatter_custom_fusion.15
  210.5 7.7 scatter_fusion
  218.2 7.7 all-to-all-start
  230.5 4.7 collective-permute-start.11
  238.1 7.7 scatter_fusion.1
  245.8 11.6 all-to-all-start.1
  261.5 9.1 reduce-window.16
  275.7 127.6 %all-reduce.14.cloned.1.call-done = bf16[256,256]{0,1:T(8,128)(2,1)} async-done(((bf16[256,256]{0,1:T(8,128)(2,1)}), bf16[256,256]{0,1:T(8,128)(2,1)}) %all-reduce.14.cloned.1.call-update) | async-done | bytes 131088 | tf_op jit(solution)/shard_map/psum | solution.py:154
  404.4 4.6 collective-permute-start.15
  415.2 13.9 collective-permute-start.17
  432.2 8.0 scatter_custom_fusion.13
  444.8 4.6 collective-permute-start.20
  449.5 8.0 scatter_custom_fusion.16
  458.5 15.0 scatter_fusion.2
  473.5 7.6 all-to-all-start.2
  487.2 15.0 scatter_fusion.3
  502.2 11.7 all-to-all-start.3
  535.0 128.0 %all-reduce.16.cloned.1.call-done = bf16[192,256]{1,0:T(8,128)(2,1)} async-done(((bf16[192,256]{1,0:T(8,128)(2,1)}), bf16[192,256]{1,0:T(8,128)(2,1)}) %all-reduce.16.cloned.1.call-update) | async-done | bytes 98320 | tf_op jit(solution)/shard_map/psum | solution.py:154
  669.5 4.6 collective-permute-start.27
  681.0 15.2 collective-permute-start.29
  705.4 4.6 collective-permute-start.32
  717.4 22.2 %scatter_fusion.4 = bf16[16,24,256]{2,1,0:T(8,128)(2,1)} fusion(bf16[16,24,256]{2,1,0:T(8,128)(2,1)} %broadcast.1392.clone.1, s32[192]{0:T(256)S(1)} %bitcast.300, bf16[192,256]{1,0:T(8,128)(2,1)S(1)} %maximum_select_fusion.4), kind=kCustom, calls=%fused_computation.14 | custom fusion | bytes 296448 | tf_op jit(solution)/shard_map/scatter | solution.py:48
  739.6 6.4 all-to-all-start.4
  751.4 4.8 collective-permute-start.34
  756.1 4.6 collective-permute-start.2
  761.5 22.1 %scatter_fusion.5 = bf16[16,24,256]{2,1,0:T(8,128)(2,1)} fusion(bf16[16,24,256]{2,1,0:T(8,128)(2,1)} %broadcast.1392.clone, s32[192]{0:T(256)S(1)} %bitcast.299, bf16[192,256]{1,0:T(8,128)(2,1)S(1)} %collective-permute-done.34), kind=kCustom, calls=%fused_computation.16 | custom fusion | bytes 296448 | tf_op jit(solution)/shard_map/scatter | solution.py:48
  783.6 11.7 all-to-all-start.5
  795.3 11.8 scatter_custom_fusion.12
  809.6 11.8 scatter_custom_fusion.17
  832.0 127.1 %all-reduce.18.cloned.1.call-done = bf16[128,256]{0,1:T(8,128)(2,1)} async-done(((bf16[128,256]{0,1:T(8,128)(2,1)}), bf16[128,256]{0,1:T(8,128)(2,1)}) %all-reduce.18.cloned.1.call-update) | async-done | bytes 65552 | tf_op jit(solution)/shard_map/psum | solution.py:154
  960.8 138.6 %all-reduce.20.cloned.1.call-done = bf16[256,256]{0,1:T(8,128)(2,1)} async-done(((bf16[256,256]{0,1:T(8,128)(2,1)}), bf16[256,256]{0,1:T(8,128)(2,1)}) %all-reduce.20.cloned.1.call-update) | async-done | bytes 131088 | tf_op jit(solution)/shard_map/psum | solution.py:216
  1102.5 24.2 %all_to_all.45 = bf16[16,24,256]{2,1,0:T(8,128)(2,1)S(1)} all-to-all(bf16[16,24,256]{2,1,0:T(8,128)(2,1)S(1)} %bitcast.302), channel_id=1, replica_groups=mesh['row'=16,'col'=32] {'row'}, dimensions={0} | all-to-all | bytes 393216 | tf_op jit(solution)/shard_map/all_to_all | solution.py:203
  1130.0 121.3 %all-reduce.22.cloned.1.call-done = bf16[192,256]{1,0:T(8,128)(2,1)} async-done(((bf16[192,256]{1,0:T(8,128)(2,1)}), bf16[192,256]{1,0:T(8,128)(2,1)}) %all-reduce.22.cloned.1.call-update) | async-done | bytes 98320 | tf_op jit(solution)/shard_map/psum | solution.py:212
  1257.8 4.6 collective-permute-start.36
  1269.4 15.2 collective-permute-start.38
  1293.8 4.6 collective-permute-start.41
  1306.3 18.2 %all_to_all.46 = bf16[16,16,256]{2,1,0:T(8,128)(2,1)S(1)} all-to-all(bf16[16,16,256]{2,1,0:T(8,128)(2,1)S(1)} %bitcast.307), channel_id=1, replica_groups=mesh['row'=16,'col'=32] {'row'}, dimensions={0} | all-to-all | bytes 262144 | tf_op jit(solution)/shard_map/all_to_all | solution.py:203
  1326.6 123.0 %all-reduce.24.cloned.1.call-done = bf16[256,256]{0,1:T(8,128)(2,1)} async-done(((bf16[256,256]{0,1:T(8,128)(2,1)}), bf16[256,256]{0,1:T(8,128)(2,1)}) %all-reduce.24.cloned.1.call-update) | async-done | bytes 131088 | tf_op jit(solution)/shard_map/psum | solution.py:212
  1450.7 4.6 collective-permute-start.43
  1461.4 13.9 collective-permute-start.45
  1483.7 4.6 collective-permute-start.48
  1490.9 19.0 %all_to_all.47 = bf16[16,8,256]{2,1,0:T(8,128)(2,1)S(1)} all-to-all(bf16[16,8,256]{2,1,0:T(8,128)(2,1)S(1)} %bitcast.308), channel_id=1, replica_groups=mesh['row'=16,'col'=32] {'row'}, dimensions={0} | all-to-all | bytes 131072 | tf_op jit(solution)/shard_map/all_to_all | solution.py:203
  1511.7 120.9 %all-reduce.26.cloned.1.call-done = bf16[256,256]{0,1:T(8,128)(2,1)} async-done(((bf16[256,256]{0,1:T(8,128)(2,1)}), bf16[256,256]{0,1:T(8,128)(2,1)}) %all-reduce.26.cloned.1.call-update) | async-done | bytes 131088 | tf_op jit(solution)/shard_map/psum | solution.py:212
  1638.6 12.4 collective-permute-start.50
  (384 shorter events, 220.3 us)
Async XLA Ops:
  7.2 172.1 %all-reduce.12.cloned.1.call-start = ((), (), s32[]{:S(2)}) async-start(), calls=%async_computation.9 | async-start | bytes 262144 | tf_op jit(solution)/shard_map/psum | solution.py:154
  7.2 40.5 %collective-permute-start.5 = (bf16[64,64]{1,0:T(8,128)(2,1)}, bf16[64,64]{1,0:T(8,128)(2,1)S(1)}, u32[]{:S(2)}, u32[]{:S(2)}) collective-permute-start(bf16[64,64]{1,0:T(8,128)(2,1)} %param.24), channel_id=1, source_target_pairs={{0,1},{1,0},{2,3},{3,2},{4,5},{5,4},{6,7},{7,6},{8,9},{9,8},{10,11... | collective-permute-start | bytes 24584 | tf_op jit(solution)/shard_map/ppermute | solution.py:10
  16.0 219.2 %collective-permute-start.12 = (bf16[128,32]{0,1:T(8,128)(2,1)}, bf16[128,32]{0,1:T(8,128)(2,1)S(1)}, u32[]{:S(2)}, u32[]{:S(2)}) collective-permute-start(bf16[128,32]{0,1:T(8,128)(2,1)} %param.23), channel_id=1, source_target_pairs={{0,1},{1,0},{2,3},{3,2},{4,5},{5,4},{6,7},{7,6},{8,9},{9,8},{10,11... | collective-permute-start | bytes 24584 | tf_op jit(solution)/shard_map/ppermute | solution.py:10
  18.0 466.7 %collective-permute-start.22 = (bf16[192,16]{0,1:T(8,128)(2,1)}, bf16[192,16]{0,1:T(8,128)(2,1)S(1)}, u32[]{:S(2)}, u32[]{:S(2)}) collective-permute-start(bf16[192,16]{0,1:T(8,128)(2,1)} %param.22), channel_id=1, source_target_pairs={{0,1},{1,0},{2,3},{3,2},{4,5},{5,4},{6,7},{7,6},{8,9},{9,8},{10,11... | collective-permute-start | bytes 18440 | tf_op jit(solution)/shard_map/ppermute | solution.py:10
  20.4 725.8 %collective-permute-start = (bf16[256,8]{0,1:T(8,128)(2,1)}, bf16[256,8]{0,1:T(8,128)(2,1)S(1)}, u32[]{:S(2)}, u32[]{:S(2)}) collective-permute-start(bf16[256,8]{0,1:T(8,128)(2,1)} %param.21), channel_id=1, source_target_pairs={{0,1},{1,0},{2,3},{3,2},{4,5},{5,4},{6,7},{7,6},{8,9},{9,8},{10,11... | collective-permute-start | bytes 12296 | tf_op jit(solution)/shard_map/ppermute | solution.py:10
  180.4 4.9 collective-permute-start.7
  185.4 16.8 %collective-permute-start.8 = (bf16[64,64]{1,0:T(8,128)(2,1)S(1)}, bf16[64,64]{1,0:T(8,128)(2,1)S(1)}, u32[]{:S(2)}, u32[]{:S(2)}) collective-permute-start(bf16[64,64]{1,0:T(8,128)(2,1)S(1)} %select_convert_fusion.14), channel_id=1, source_target_pairs={{0,1},{1,0},{2,3},{3,2},{4,5},{5,4},{6,7},{7,6},{8,9},{9,8},{10,11... | collective-permute-start | bytes 24584 | tf_op jit(solution)/shard_map/ppermute | solution.py:10
  218.2 27.6 %all-to-all-start = ((bf16[16,8,256]{2,1,0:T(8,128)(2,1)}), bf16[16,8,256]{2,1,0:T(8,128)(2,1)S(1)}, u32[]{:S(2)}, u32[]{:S(2)}) async-start(bf16[16,8,256]{2,1,0:T(8,128)(2,1)} %scatter_fusion), calls=%async_computation | async-start | bytes 131072 | tf_op jit(solution)/shard_map/all_to_all | solution.py:170
  230.5 6.9 collective-permute-start.11
  235.2 22.2 %collective-permute-start.13 = (bf16[128,64]{0,1:T(8,128)(2,1)S(1)}, bf16[128,64]{0,1:T(8,128)(2,1)S(1)}, u32[]{:S(2)}, u32[]{:S(2)}) collective-permute-start(bf16[128,64]{0,1:T(8,128)(2,1)S(1)} %maximum_select_fusion.28), channel_id=1, source_target_pairs={{0,2},{1,3},{2,0},{3,1},{4,6},{5,7},{6,4},{7,5},{8,10},{9,11},{10,... | collective-permute-start | bytes 49160 | tf_op jit(solution)/shard_map/ppermute | solution.py:10
  245.8 26.7 %all-to-all-start.1 = ((bf16[16,8,256]{2,1,0:T(8,128)(2,1)}), bf16[16,8,256]{2,1,0:T(8,128)(2,1)S(1)}, u32[]{:S(2)}, u32[]{:S(2)}) async-start(bf16[16,8,256]{2,1,0:T(8,128)(2,1)} %scatter_fusion.1), calls=%async_computation.1 | async-start | bytes 131072 | tf_op jit(solution)/shard_map/all_to_all | solution.py:177
  257.4 145.9 %all-reduce.14.cloned.1.call-start = ((), (), s32[]{:S(2)}) async-start(), calls=%async_computation.10 | async-start | bytes 262144 | tf_op jit(solution)/shard_map/psum | solution.py:154
  257.5 16.6 collective-permute-start.14
  404.4 6.2 collective-permute-start.15
  415.2 14.7 collective-permute-start.17
  429.9 10.4 collective-permute-start.18
  444.8 12.9 collective-permute-start.20
  473.5 28.7 %all-to-all-start.2 = ((bf16[16,16,256]{2,1,0:T(8,128)(2,1)}), bf16[16,16,256]{2,1,0:T(8,128)(2,1)S(1)}, u32[]{:S(2)}, u32[]{:S(2)}) async-start(bf16[16,16,256]{2,1,0:T(8,128)(2,1)} %scatter_fusion.2), calls=%async_computation.2 | async-start | bytes 262144 | tf_op jit(solution)/shard_map/all_to_all | solution.py:170
  481.4 5.0 collective-permute-start.21
  502.2 28.9 %all-to-all-start.3 = ((bf16[16,16,256]{2,1,0:T(8,128)(2,1)}), bf16[16,16,256]{2,1,0:T(8,128)(2,1)S(1)}, u32[]{:S(2)}, u32[]{:S(2)}) async-start(bf16[16,16,256]{2,1,0:T(8,128)(2,1)} %scatter_fusion.3), calls=%async_computation.3 | async-start | bytes 262144 | tf_op jit(solution)/shard_map/all_to_all | solution.py:177
  513.9 149.2 %all-reduce.16.cloned.1.call-start = ((), (), s32[]{:S(2)}) async-start(), calls=%async_computation.11 | async-start | bytes 196608 | tf_op jit(solution)/shard_map/psum | solution.py:154
  514.0 4.8 collective-permute-start.23
  518.9 6.6 collective-permute-start.24
  525.6 7.6 collective-permute-start.25
  664.1 5.2 collective-permute-start.26
  669.5 6.3 collective-permute-start.27
  681.0 16.1 collective-permute-start.29
  705.4 6.3 collective-permute-start.32
  739.6 44.0 %all-to-all-start.4 = ((bf16[16,24,256]{2,1,0:T(8,128)(2,1)}), bf16[16,24,256]{2,1,0:T(8,128)(2,1)S(1)}, u32[]{:S(2)}, u32[]{:S(2)}) async-start(bf16[16,24,256]{2,1,0:T(8,128)(2,1)} %scatter_fusion.4), calls=%async_computation.4 | async-start | bytes 393216 | tf_op jit(solution)/shard_map/all_to_all | solution.py:170
  751.4 9.4 collective-permute-start.34
  756.1 51.1 %collective-permute-start.2 = (bf16[256,32]{1,0:T(8,128)(2,1)S(1)}, bf16[256,32]{1,0:T(8,128)(2,1)S(1)}, u32[]{:S(2)}, u32[]{:S(2)}) collective-permute-start(bf16[256,32]{1,0:T(8,128)(2,1)S(1)} %broadcast_select_fusion), channel_id=1, source_target_pairs={{0,4},{1,5},{2,6},{3,7},{4,0},{5,1},{6,2},{7,3},{8,12},{9,13},{10,... | collective-permute-start | bytes 49160 | tf_op jit(solution)/shard_map/ppermute | solution.py:10
  783.6 44.6 %all-to-all-start.5 = ((bf16[16,24,256]{2,1,0:T(8,128)(2,1)}), bf16[16,24,256]{2,1,0:T(8,128)(2,1)S(1)}, u32[]{:S(2)}, u32[]{:S(2)}) async-start(bf16[16,24,256]{2,1,0:T(8,128)(2,1)} %scatter_fusion.5), calls=%async_computation.5 | async-start | bytes 393216 | tf_op jit(solution)/shard_map/all_to_all | solution.py:177
  795.3 163.8 %all-reduce.18.cloned.1.call-start = ((), (), s32[]{:S(2)}) async-start(), calls=%async_computation.12 | async-start | bytes 131072 | tf_op jit(solution)/shard_map/psum | solution.py:154
  807.3 14.1 collective-permute-start.3
  821.6 9.5 collective-permute-start.4
  831.9 267.5 %all-reduce.20.cloned.1.call-start = ((), (), s32[]{:S(2)}) async-start(), calls=%async_computation.13 | async-start | bytes 262144 | tf_op jit(solution)/shard_map/psum | solution.py:216
  960.8 290.6 %all-reduce.22.cloned.1.call-start = ((), (), s32[]{:S(2)}) async-start(), calls=%async_computation.14 | async-start | bytes 196608 | tf_op jit(solution)/shard_map/psum | solution.py:212
  1130.0 319.6 %all-reduce.24.cloned.1.call-start = ((), (), s32[]{:S(2)}) async-start(), calls=%async_computation.15 | async-start | bytes 262144 | tf_op jit(solution)/shard_map/psum | solution.py:212
  1252.5 5.2 collective-permute-start.35
  1257.8 6.3 collective-permute-start.36
  1269.4 16.1 collective-permute-start.38
  1293.8 6.3 collective-permute-start.41
  1326.6 306.0 %all-reduce.26.cloned.1.call-start = ((), (), s32[]{:S(2)}) async-start(), calls=%async_computation.16 | async-start | bytes 262144 | tf_op jit(solution)/shard_map/psum | solution.py:212
  1450.7 6.2 collective-permute-start.43
  1461.4 14.7 collective-permute-start.45
  1483.7 6.2 collective-permute-start.48
  1633.6 4.9 collective-permute-start.49
  1638.6 14.3 collective-permute-start.50
  (40 other events, 1395.3 us)
Sparse Core Ops, SparseCore 0:
  53.8 125.3 all-reduce.11
  275.8 127.4 all-reduce.13
  535.0 128.0 all-reduce.15
  832.1 126.9 all-reduce.17
  962.1 137.2 all-reduce.19
  1130.1 121.2 all-reduce.21
  1326.7 122.8 all-reduce.23
  1511.8 120.6 all-reduce.25
where the time goes:
time: 1670 us; the launch traced here: 1660 us
  waiting for transfers between devices  1060 us (63%)
  starting transfers between devices  293 us (18%)
  local copies, waits for them, and re-layouts  168 us (10%)
  blocking collectives  61.5 us (4%)
  other arithmetic  46.3 us (3%)
    psum x4, waiting for transfers between devices, per_device(): solved = lax.psum(partial_value.astype(jnp.bfloat16), 'row')  507 us
    psum x3, waiting for transfers between devices, per_device(): lax.psum(coupling_term.astype(jnp.bfloat16), 'row').astype(jnp.float32)  365 us
    ppermute x51, starting transfers between devices, swapped(): return lax.ppermute(value, axis, pairs)  236 us
    psum x1, waiting for transfers between devices, per_device(): summed = lax.psum(contribution.astype(jnp.bfloat16), 'col')  139 us
    scatter x6, local copies, waits for them, and re-layouts, pack_rows(): return buffer.at[local_target, local_slots].set(values)  89.7 us
    all_to_all x3, blocking collectives, per_device(): lax.all_to_all(parent_rows[own_lookup], 'row', split_axis=0, concat_axis=...  61.5 us
    unnamed x56, local copies, waits for them, and re-layouts  56.3 us
    ppermute x51, waiting for transfers between devices, swapped(): return lax.ppermute(value, axis, pairs)  50.9 us
  transfers between devices with their start and end apart: 65, of which 42 were waited for; matrix products, arithmetic and copies ran while one was open for 12% of the time, Pallas kernels for 0%

commit v1 on v0

--- a/solution.py
+++ b/solution.py
@@ -151,7 +151,8 @@
             )
             own_update = lax.optimization_barrier(incoming[sep_rows:].astype(jnp.bfloat16))
         partial_value = jnp.dot(inverses[tree_level], separator, preferred_element_type=jnp.float32)
-        solved = lax.psum(partial_value.astype(jnp.bfloat16), "row")
+        xin = partial_value.astype(jnp.bfloat16)
+        solved = lax.all_gather(xin, "row").sum(axis=0)
         pivots[tree_level] = solved
         if tree_level > 0:
             coupled = jnp.dot(couplings[tree_level], solved, preferred_element_type=jnp.float32)

time: 1670 us -> 1400 us (0.84)
  waiting for transfers between devices: 1060 us -> 778 us
    psum x4 -> x0, waiting for transfers between devices: 507 us -> none  [per_device(): solved = lax.psum(partial_value.astype(jnp.bfloat16), 'row')]
    all_gather x0 -> x4, waiting for transfers between devices: none -> 219 us  [per_device(): solved = lax.all_gather(xin, 'row').sum(axis=0)]
    unnamed x56 -> x49, local copies, waits for them, and re-layouts: 56.3 us -> 56.1 us
  transfers between devices with their start and end apart: 65 -> 65, of which waited for: 42 -> 45; matrix products, arithmetic and copies ran while one was open for 12% -> 15% of each run, Pallas kernels for 0% -> 0%
where the time goes in v1:
time: 1400 us; the launch traced here: 1390 us
  waiting for transfers between devices  778 us (56%)
  starting transfers between devices  300 us (21%)
  local copies, waits for them, and re-layouts  167 us (12%)
  blocking collectives  61.5 us (4%)
  other arithmetic  52.2 us (4%)
  between operations  16.3 us (1%)
    psum x3, waiting for transfers between devices, per_device(): lax.psum(coupling_term.astype(jnp.bfloat16), 'row').astype(jnp.float32)  365 us
    ppermute x51, starting transfers between devices, swapped(): return lax.ppermute(value, axis, pairs)  243 us
    all_gather x4, waiting for transfers between devices, per_device(): solved = lax.all_gather(xin, 'row').sum(axis=0)  219 us
    psum x1, waiting for transfers between devices, per_device(): summed = lax.psum(contribution.astype(jnp.bfloat16), 'col')  138 us
    scatter x6, local copies, waits for them, and re-layouts, pack_rows(): return buffer.at[local_target, local_slots].set(values)  89.7 us
    all_to_all x3, blocking collectives, per_device(): lax.all_to_all(parent_rows[own_lookup], 'row', split_axis=0, concat_axis=...  61.5 us
    unnamed x49, local copies, waits for them, and re-layouts  56.1 us
    ppermute x51, waiting for transfers between devices, swapped(): return lax.ppermute(value, axis, pairs)  47.9 us
  transfers between devices with their start and end apart: 65, of which 45 were waited for; matrix products, arithmetic and copies ran while one was open for 15% of the time, Pallas kernels for 0%

profile of v1, /device:TPU:1, one launch (start us, length us, event | category | flops | bytes accessed | tf_op | source)
XLA Modules:
  0.0 1386.6 jit_solution(16436757630806562708)
XLA Ops:
  7.2 8.8 collective-permute-start.5
  34.0 58.9 %all-gather.9.cloned.1.call-done = bf16[4096,256]{0,1:T(8,128)(2,1)} async-done(((bf16[256,256]{0,1:T(8,128)(2,1)}), bf16[4096,256]{0,1:T(8,128)(2,1)}) %all-gather.9.cloned.1.call-update) | async-done | bytes 2097168 | tf_op jit(solution)/shard_map/all_gather | solution.py:155
  101.1 13.7 collective-permute-start.8
  127.6 7.7 scatter_fusion
  135.3 7.1 all-to-all-start
  155.2 7.7 scatter_fusion.1
  162.8 11.6 all-to-all-start.1
  178.5 7.5 all-to-all-done.1
  188.6 5.9 collective-permute-start.22
  204.2 48.8 %all-gather.11.cloned.1.call-done = bf16[4096,256]{0,1:T(8,128)(2,1)} async-done(((bf16[256,256]{0,1:T(8,128)(2,1)}), bf16[4096,256]{0,1:T(8,128)(2,1)}) %all-gather.11.cloned.1.call-update) | async-done | bytes 2097168 | tf_op jit(solution)/shard_map/all_gather | solution.py:155
  256.7 4.6 collective-permute-start.15
  267.4 14.8 %collective-permute-start.17 = (bf16[128,32]{0,1:T(8,128)(2,1)S(1)}, bf16[128,32]{0,1:T(8,128)(2,1)S(1)}, u32[]{:S(2)}, u32[]{:S(2)}) collective-permute-start(bf16[128,32]{0,1:T(8,128)(2,1)S(1)} %select_convert_fusion.17), channel_id=1, source_target_pairs={{0,1},{1,0},{2,3},{3,2},{4,5},{5,4},{6,7},{7,6},{8,9},{9,8},{10,11... | collective-permute-start | bytes 24584 | tf_op jit(solution)/shard_map/ppermute | solution.py:10
  290.6 4.6 collective-permute-start.20
  295.3 8.0 scatter_custom_fusion.13
  304.3 15.0 %scatter_fusion.2 = bf16[16,16,256]{2,1,0:T(8,128)(2,1)} fusion(bf16[16,16,256]{2,1,0:T(8,128)(2,1)} %broadcast.1409.clone.1, s32[128]{0:T(128)S(1)} %get-tuple-element.77, bf16[128,256]{1,0:T(8,128)(2,1)S(1)} %copy.212), kind=kCustom, calls=%fused_computation.10 | custom fusion | bytes 197632 | tf_op jit(solution)/shard_map/scatter | solution.py:48
  319.3 7.2 all-to-all-start.2
  326.6 8.0 scatter_custom_fusion.16
  341.2 15.0 %scatter_fusion.3 = bf16[16,16,256]{2,1,0:T(8,128)(2,1)} fusion(bf16[16,16,256]{2,1,0:T(8,128)(2,1)} %broadcast.1409.clone, s32[128]{0:T(128)S(1)} %fusion.156, bf16[128,256]{1,0:T(8,128)(2,1)S(1)} %copy.222), kind=kCustom, calls=%fused_computation.12 | custom fusion | bytes 197632 | tf_op jit(solution)/shard_map/scatter | solution.py:48
  356.2 11.5 all-to-all-start.3
  382.8 9.1 reduce-window.14
  392.9 9.1 reduce-window.16
  402.9 45.3 %all-gather.13.cloned.1.call-done = bf16[3072,256]{1,0:T(8,128)(2,1)} async-done(((bf16[192,256]{1,0:T(8,128)(2,1)}), bf16[3072,256]{1,0:T(8,128)(2,1)}) %all-gather.13.cloned.1.call-update) | async-done | bytes 1572880 | tf_op jit(solution)/shard_map/all_gather | solution.py:155
  455.4 4.7 collective-permute-start.27
  467.0 15.4 %collective-permute-start.29 = (bf16[192,16]{1,0:T(8,128)(2,1)S(1)}, bf16[192,16]{1,0:T(8,128)(2,1)S(1)}, u32[]{:S(2)}, u32[]{:S(2)}) collective-permute-start(bf16[192,16]{1,0:T(8,128)(2,1)S(1)} %select_convert_fusion.4), channel_id=1, source_target_pairs={{0,1},{1,0},{2,3},{3,2},{4,5},{5,4},{6,7},{7,6},{8,9},{9,8},{10,11... | collective-permute-start | bytes 18440 | tf_op jit(solution)/shard_map/ppermute | solution.py:10
  491.5 4.7 collective-permute-start.32
  503.5 22.2 %scatter_fusion.4 = bf16[16,24,256]{2,1,0:T(8,128)(2,1)} fusion(bf16[16,24,256]{2,1,0:T(8,128)(2,1)} %broadcast.1392.clone.1, s32[192]{0:T(256)S(1)} %bitcast.316, bf16[192,256]{1,0:T(8,128)(2,1)S(1)} %maximum_select_fusion.4), kind=kCustom, calls=%fused_computation.14 | custom fusion | bytes 296448 | tf_op jit(solution)/shard_map/scatter | solution.py:48
  525.7 7.5 all-to-all-start.4
  538.0 4.9 collective-permute-start.34
  542.9 4.5 collective-permute-start.2
  548.1 22.1 %scatter_fusion.5 = bf16[16,24,256]{2,1,0:T(8,128)(2,1)} fusion(bf16[16,24,256]{2,1,0:T(8,128)(2,1)} %broadcast.1392.clone, s32[192]{0:T(256)S(1)} %bitcast.315, bf16[192,256]{1,0:T(8,128)(2,1)S(1)} %collective-permute-done.34), kind=kCustom, calls=%fused_computation.16 | custom fusion | bytes 296448 | tf_op jit(solution)/shard_map/scatter | solution.py:48
  570.2 11.7 all-to-all-start.5
  582.4 11.8 scatter_custom_fusion.12
  596.6 11.8 scatter_custom_fusion.17
  618.9 65.8 %all-gather.15.cloned.1.call-done = bf16[2048,256]{0,1:T(8,128)(2,1)} async-done(((bf16[128,256]{0,1:T(8,128)(2,1)}), bf16[2048,256]{0,1:T(8,128)(2,1)}) %all-gather.15.cloned.1.call-update) | async-done | bytes 1048592 | tf_op jit(solution)/shard_map/all_gather | solution.py:155
  687.7 137.6 %all-reduce.8.cloned.1.call-done = bf16[256,256]{0,1:T(8,128)(2,1)} async-done(((bf16[256,256]{0,1:T(8,128)(2,1)}), bf16[256,256]{0,1:T(8,128)(2,1)}) %all-reduce.8.cloned.1.call-update) | async-done | bytes 131088 | tf_op jit(solution)/shard_map/psum | solution.py:217
  828.4 24.2 %all_to_all.45 = bf16[16,24,256]{2,1,0:T(8,128)(2,1)S(1)} all-to-all(bf16[16,24,256]{2,1,0:T(8,128)(2,1)S(1)} %bitcast.322), channel_id=1, replica_groups=mesh['row'=16,'col'=32] {'row'}, dimensions={0} | all-to-all | bytes 393216 | tf_op jit(solution)/shard_map/all_to_all | solution.py:204
  855.9 121.3 %all-reduce.10.cloned.1.call-done = bf16[192,256]{1,0:T(8,128)(2,1)} async-done(((bf16[192,256]{1,0:T(8,128)(2,1)}), bf16[192,256]{1,0:T(8,128)(2,1)}) %all-reduce.10.cloned.1.call-update) | async-done | bytes 98320 | tf_op jit(solution)/shard_map/psum | solution.py:213
  983.7 4.6 collective-permute-start.36
  995.3 15.2 %collective-permute-start.38 = (bf16[192,16]{1,0:T(8,128)(2,1)S(1)}, bf16[192,16]{1,0:T(8,128)(2,1)S(1)}, u32[]{:S(2)}, u32[]{:S(2)}) collective-permute-start(bf16[192,16]{1,0:T(8,128)(2,1)S(1)} %select_convert_fusion), channel_id=1, source_target_pairs={{0,1},{1,0},{2,3},{3,2},{4,5},{5,4},{6,7},{7,6},{8,9},{9,8},{10,11... | collective-permute-start | bytes 18440 | tf_op jit(solution)/shard_map/ppermute | solution.py:10
  1019.7 4.6 collective-permute-start.41
  1032.2 18.2 %all_to_all.46 = bf16[16,16,256]{2,1,0:T(8,128)(2,1)S(1)} all-to-all(bf16[16,16,256]{2,1,0:T(8,128)(2,1)S(1)} %bitcast.327), channel_id=1, replica_groups=mesh['row'=16,'col'=32] {'row'}, dimensions={0} | all-to-all | bytes 262144 | tf_op jit(solution)/shard_map/all_to_all | solution.py:204
  1052.5 123.0 %all-reduce.12.cloned.1.call-done = bf16[256,256]{0,1:T(8,128)(2,1)} async-done(((bf16[256,256]{0,1:T(8,128)(2,1)}), bf16[256,256]{0,1:T(8,128)(2,1)}) %all-reduce.12.cloned.1.call-update) | async-done | bytes 131088 | tf_op jit(solution)/shard_map/psum | solution.py:213
  1176.6 4.6 collective-permute-start.43
  1187.3 13.9 %collective-permute-start.45 = (bf16[128,32]{0,1:T(8,128)(2,1)S(1)}, bf16[128,32]{0,1:T(8,128)(2,1)S(1)}, u32[]{:S(2)}, u32[]{:S(2)}) collective-permute-start(bf16[128,32]{0,1:T(8,128)(2,1)S(1)} %select_convert_fusion.16), channel_id=1, source_target_pairs={{0,1},{1,0},{2,3},{3,2},{4,5},{5,4},{6,7},{7,6},{8,9},{9,8},{10,11... | collective-permute-start | bytes 24584 | tf_op jit(solution)/shard_map/ppermute | solution.py:10
  1209.6 4.6 collective-permute-start.48
  1216.8 19.0 %all_to_all.47 = bf16[16,8,256]{2,1,0:T(8,128)(2,1)S(1)} all-to-all(bf16[16,8,256]{2,1,0:T(8,128)(2,1)S(1)} %bitcast.328), channel_id=1, replica_groups=mesh['row'=16,'col'=32] {'row'}, dimensions={0} | all-to-all | bytes 131072 | tf_op jit(solution)/shard_map/all_to_all | solution.py:204
  1237.6 120.9 %all-reduce.14.cloned.1.call-done = bf16[256,256]{0,1:T(8,128)(2,1)} async-done(((bf16[256,256]{0,1:T(8,128)(2,1)}), bf16[256,256]{0,1:T(8,128)(2,1)}) %all-reduce.14.cloned.1.call-update) | async-done | bytes 131088 | tf_op jit(solution)/shard_map/psum | solution.py:213
  1364.5 12.4 collective-permute-start.50
  (381 shorter events, 228.8 us)
Async XLA Ops:
  7.2 85.7 %all-gather.9.cloned.1.call-start = ((), (), s32[]{:S(2)}) async-start(), calls=%async_computation.13 | async-start | bytes 2228224 | tf_op jit(solution)/shard_map/all_gather | solution.py:155
  7.2 9.8 collective-permute-start.5
  24.1 118.5 %collective-permute-start.12 = (bf16[128,32]{0,1:T(8,128)(2,1)}, bf16[128,32]{0,1:T(8,128)(2,1)S(1)}, u32[]{:S(2)}, u32[]{:S(2)}) collective-permute-start(bf16[128,32]{0,1:T(8,128)(2,1)} %param.23), channel_id=1, source_target_pairs={{0,1},{1,0},{2,3},{3,2},{4,5},{5,4},{6,7},{7,6},{8,9},{9,8},{10,11... | collective-permute-start | bytes 24584 | tf_op jit(solution)/shard_map/ppermute | solution.py:10
  101.1 18.1 %collective-permute-start.8 = (bf16[64,64]{1,0:T(8,128)(2,1)S(1)}, bf16[64,64]{1,0:T(8,128)(2,1)S(1)}, u32[]{:S(2)}, u32[]{:S(2)}) collective-permute-start(bf16[64,64]{1,0:T(8,128)(2,1)S(1)} %select_convert_fusion.14), channel_id=1, source_target_pairs={{0,1},{1,0},{2,3},{3,2},{4,5},{5,4},{6,7},{7,6},{8,9},{9,8},{10,11... | collective-permute-start | bytes 24584 | tf_op jit(solution)/shard_map/ppermute | solution.py:10
  135.3 27.6 %all-to-all-start = ((bf16[16,8,256]{2,1,0:T(8,128)(2,1)}), bf16[16,8,256]{2,1,0:T(8,128)(2,1)S(1)}, u32[]{:S(2)}, u32[]{:S(2)}) async-start(bf16[16,8,256]{2,1,0:T(8,128)(2,1)} %scatter_fusion), calls=%async_computation | async-start | bytes 131072 | tf_op jit(solution)/shard_map/all_to_all | solution.py:171
  142.5 32.0 %collective-permute-start.13 = (bf16[128,64]{0,1:T(8,128)(2,1)S(1)}, bf16[128,64]{0,1:T(8,128)(2,1)S(1)}, u32[]{:S(2)}, u32[]{:S(2)}) collective-permute-start(bf16[128,64]{0,1:T(8,128)(2,1)S(1)} %maximum_select_fusion.28), channel_id=1, source_target_pairs={{0,2},{1,3},{2,0},{3,1},{4,6},{5,7},{6,4},{7,5},{8,10},{9,11},{10,... | collective-permute-start | bytes 49160 | tf_op jit(solution)/shard_map/ppermute | solution.py:10
  145.7 8.9 collective-permute-start.11
  162.8 23.2 %all-to-all-start.1 = ((bf16[16,8,256]{2,1,0:T(8,128)(2,1)}), bf16[16,8,256]{2,1,0:T(8,128)(2,1)S(1)}, u32[]{:S(2)}, u32[]{:S(2)}) async-start(bf16[16,8,256]{2,1,0:T(8,128)(2,1)} %scatter_fusion.1), calls=%async_computation.1 | async-start | bytes 131072 | tf_op jit(solution)/shard_map/all_to_all | solution.py:178
  174.5 78.6 %all-gather.11.cloned.1.call-start = ((), (), s32[]{:S(2)}) async-start(), calls=%async_computation.14 | async-start | bytes 2228224 | tf_op jit(solution)/shard_map/all_gather | solution.py:155
  174.5 13.2 collective-permute-start.14
  188.6 146.1 %collective-permute-start.22 = (bf16[192,16]{0,1:T(8,128)(2,1)S(1)}, bf16[192,16]{0,1:T(8,128)(2,1)S(1)}, u32[]{:S(2)}, u32[]{:S(2)}) collective-permute-start(bf16[192,16]{0,1:T(8,128)(2,1)S(1)} %copy-done.11), channel_id=1, source_target_pairs={{0,1},{1,0},{2,3},{3,2},{4,5},{5,4},{6,7},{7,6},{8,9},{9,8},{10,11... | collective-permute-start | bytes 18440 | tf_op jit(solution)/shard_map/ppermute | solution.py:10
  194.5 338.8 %collective-permute-start = (bf16[256,8]{0,1:T(8,128)(2,1)S(1)}, bf16[256,8]{0,1:T(8,128)(2,1)S(1)}, u32[]{:S(2)}, u32[]{:S(2)}) collective-permute-start(bf16[256,8]{0,1:T(8,128)(2,1)S(1)} %copy-done.12), channel_id=1, source_target_pairs={{0,1},{1,0},{2,3},{3,2},{4,5},{5,4},{6,7},{7,6},{8,9},{9,8},{10,11... | collective-permute-start | bytes 12296 | tf_op jit(solution)/shard_map/ppermute | solution.py:10
  256.7 6.2 collective-permute-start.15
  267.4 15.6 %collective-permute-start.17 = (bf16[128,32]{0,1:T(8,128)(2,1)S(1)}, bf16[128,32]{0,1:T(8,128)(2,1)S(1)}, u32[]{:S(2)}, u32[]{:S(2)}) collective-permute-start(bf16[128,32]{0,1:T(8,128)(2,1)S(1)} %select_convert_fusion.17), channel_id=1, source_target_pairs={{0,1},{1,0},{2,3},{3,2},{4,5},{5,4},{6,7},{7,6},{8,9},{9,8},{10,11... | collective-permute-start | bytes 24584 | tf_op jit(solution)/shard_map/ppermute | solution.py:10
  290.6 12.9 collective-permute-start.20
  319.3 37.0 %all-to-all-start.2 = ((bf16[16,16,256]{2,1,0:T(8,128)(2,1)}), bf16[16,16,256]{2,1,0:T(8,128)(2,1)S(1)}, u32[]{:S(2)}, u32[]{:S(2)}) async-start(bf16[16,16,256]{2,1,0:T(8,128)(2,1)} %scatter_fusion.2), calls=%async_computation.2 | async-start | bytes 262144 | tf_op jit(solution)/shard_map/all_to_all | solution.py:171
  335.0 5.5 collective-permute-start.21
  338.2 29.6 %collective-permute-start.23 = (bf16[192,32]{1,0:T(8,128)(2,1)S(1)}, bf16[192,32]{1,0:T(8,128)(2,1)S(1)}, u32[]{:S(2)}, u32[]{:S(2)}) collective-permute-start(bf16[192,32]{1,0:T(8,128)(2,1)S(1)} %broadcast_select_fusion.1), channel_id=1, source_target_pairs={{0,2},{1,3},{2,0},{3,1},{4,6},{5,7},{6,4},{7,5},{8,10},{9,11},{10,... | collective-permute-start | bytes 36872 | tf_op jit(solution)/shard_map/ppermute | solution.py:10
  356.2 23.5 %all-to-all-start.3 = ((bf16[16,16,256]{2,1,0:T(8,128)(2,1)}), bf16[16,16,256]{2,1,0:T(8,128)(2,1)S(1)}, u32[]{:S(2)}, u32[]{:S(2)}) async-start(bf16[16,16,256]{2,1,0:T(8,128)(2,1)} %scatter_fusion.3), calls=%async_computation.3 | async-start | bytes 262144 | tf_op jit(solution)/shard_map/all_to_all | solution.py:178
  367.8 80.5 %all-gather.13.cloned.1.call-start = ((), (), s32[]{:S(2)}) async-start(), calls=%async_computation.15 | async-start | bytes 1671168 | tf_op jit(solution)/shard_map/all_gather | solution.py:155
  368.0 6.3 collective-permute-start.24
  374.4 7.5 collective-permute-start.25
  450.1 5.2 collective-permute-start.26
  455.4 6.3 collective-permute-start.27
  467.0 16.3 %collective-permute-start.29 = (bf16[192,16]{1,0:T(8,128)(2,1)S(1)}, bf16[192,16]{1,0:T(8,128)(2,1)S(1)}, u32[]{:S(2)}, u32[]{:S(2)}) collective-permute-start(bf16[192,16]{1,0:T(8,128)(2,1)S(1)} %select_convert_fusion.4), channel_id=1, source_target_pairs={{0,1},{1,0},{2,3},{3,2},{4,5},{5,4},{6,7},{7,6},{8,9},{9,8},{10,11... | collective-permute-start | bytes 18440 | tf_op jit(solution)/shard_map/ppermute | solution.py:10
  491.5 6.3 collective-permute-start.32
  498.0 4.8 collective-permute-start.33
  525.7 44.5 %all-to-all-start.4 = ((bf16[16,24,256]{2,1,0:T(8,128)(2,1)}), bf16[16,24,256]{2,1,0:T(8,128)(2,1)S(1)}, u32[]{:S(2)}, u32[]{:S(2)}) async-start(bf16[16,24,256]{2,1,0:T(8,128)(2,1)} %scatter_fusion.4), calls=%async_computation.4 | async-start | bytes 393216 | tf_op jit(solution)/shard_map/all_to_all | solution.py:171
  538.0 9.4 collective-permute-start.34
  542.9 51.4 %collective-permute-start.2 = (bf16[256,32]{1,0:T(8,128)(2,1)S(1)}, bf16[256,32]{1,0:T(8,128)(2,1)S(1)}, u32[]{:S(2)}, u32[]{:S(2)}) collective-permute-start(bf16[256,32]{1,0:T(8,128)(2,1)S(1)} %broadcast_select_fusion), channel_id=1, source_target_pairs={{0,4},{1,5},{2,6},{3,7},{4,0},{5,1},{6,2},{7,3},{8,12},{9,13},{10,... | collective-permute-start | bytes 49160 | tf_op jit(solution)/shard_map/ppermute | solution.py:10
  570.2 44.9 %all-to-all-start.5 = ((bf16[16,24,256]{2,1,0:T(8,128)(2,1)}), bf16[16,24,256]{2,1,0:T(8,128)(2,1)S(1)}, u32[]{:S(2)}, u32[]{:S(2)}) async-start(bf16[16,24,256]{2,1,0:T(8,128)(2,1)} %scatter_fusion.5), calls=%async_computation.5 | async-start | bytes 393216 | tf_op jit(solution)/shard_map/all_to_all | solution.py:178
  581.9 102.8 %all-gather.15.cloned.1.call-start = ((), (), s32[]{:S(2)}) async-start(), calls=%async_computation.16 | async-start | bytes 1114112 | tf_op jit(solution)/shard_map/all_gather | solution.py:155
  594.4 14.1 %collective-permute-start.3 = (bf16[256,64]{1,0:T(8,128)(2,1)S(1)}, bf16[256,64]{1,0:T(8,128)(2,1)S(1)}, u32[]{:S(2)}, u32[]{:S(2)}) collective-permute-start(bf16[256,64]{1,0:T(8,128)(2,1)S(1)} %maximum_select_fusion.6), channel_id=1, source_target_pairs={{0,8},{1,9},{2,10},{3,11},{4,12},{5,13},{6,14},{7,15},{8,0},{9,1},... | collective-permute-start | bytes 98312 | tf_op jit(solution)/shard_map/ppermute | solution.py:10
  608.6 9.3 collective-permute-start.4
  618.9 206.5 %all-reduce.8.cloned.1.call-start = ((), (), s32[]{:S(2)}) async-start(), calls=%async_computation.9 | async-start | bytes 262144 | tf_op jit(solution)/shard_map/psum | solution.py:217
  687.6 289.6 %all-reduce.10.cloned.1.call-start = ((), (), s32[]{:S(2)}) async-start(), calls=%async_computation.10 | async-start | bytes 196608 | tf_op jit(solution)/shard_map/psum | solution.py:213
  855.9 319.6 %all-reduce.12.cloned.1.call-start = ((), (), s32[]{:S(2)}) async-start(), calls=%async_computation.11 | async-start | bytes 262144 | tf_op jit(solution)/shard_map/psum | solution.py:213
  978.4 5.2 collective-permute-start.35
  983.7 6.3 collective-permute-start.36
  995.3 16.1 %collective-permute-start.38 = (bf16[192,16]{1,0:T(8,128)(2,1)S(1)}, bf16[192,16]{1,0:T(8,128)(2,1)S(1)}, u32[]{:S(2)}, u32[]{:S(2)}) collective-permute-start(bf16[192,16]{1,0:T(8,128)(2,1)S(1)} %select_convert_fusion), channel_id=1, source_target_pairs={{0,1},{1,0},{2,3},{3,2},{4,5},{5,4},{6,7},{7,6},{8,9},{9,8},{10,11... | collective-permute-start | bytes 18440 | tf_op jit(solution)/shard_map/ppermute | solution.py:10
  1019.7 6.3 collective-permute-start.41
  1026.1 4.8 collective-permute-start.42
  1052.5 305.9 %all-reduce.14.cloned.1.call-start = ((), (), s32[]{:S(2)}) async-start(), calls=%async_computation.12 | async-start | bytes 262144 | tf_op jit(solution)/shard_map/psum | solution.py:213
  1176.6 6.2 collective-permute-start.43
  1187.3 14.7 %collective-permute-start.45 = (bf16[128,32]{0,1:T(8,128)(2,1)S(1)}, bf16[128,32]{0,1:T(8,128)(2,1)S(1)}, u32[]{:S(2)}, u32[]{:S(2)}) collective-permute-start(bf16[128,32]{0,1:T(8,128)(2,1)S(1)} %select_convert_fusion.16), channel_id=1, source_target_pairs={{0,1},{1,0},{2,3},{3,2},{4,5},{5,4},{6,7},{7,6},{8,9},{9,8},{10,11... | collective-permute-start | bytes 24584 | tf_op jit(solution)/shard_map/ppermute | solution.py:10
  1209.6 6.2 collective-permute-start.48
  1359.5 4.9 collective-permute-start.49
  1364.5 14.3 %collective-permute-start.50 = (bf16[64,64]{1,0:T(8,128)(2,1)S(1)}, bf16[64,64]{1,0:T(8,128)(2,1)S(1)}, u32[]{:S(2)}, u32[]{:S(2)}) collective-permute-start(bf16[64,64]{1,0:T(8,128)(2,1)S(1)} %select_convert_fusion.10), channel_id=1, source_target_pairs={{0,1},{1,0},{2,3},{3,2},{4,5},{5,4},{6,7},{7,6},{8,9},{9,8},{10,11... | collective-permute-start | bytes 24584 | tf_op jit(solution)/shard_map/ppermute | solution.py:10
  (35 other events, 1519.3 us)
Sparse Core Ops, SparseCore 0:
  24.2 68.6 all-gather.8
  188.7 64.2 all-gather.10
  382.8 65.3 all-gather.12
  619.0 65.7 all-gather.14
  687.8 137.4 all-reduce.7
  856.0 121.2 all-reduce.9
  1052.6 122.8 all-reduce.11
  1237.7 120.6 all-reduce.13
